TPU v7x, 32 devices: a whole 2x2x4 slice. The times are simulated.
32 devices in a mesh: groups: 2 (over x), rows: 16 (over z, y, core).
Axes of the slice: x: 2, y: 2, z: 4, core: 2. Of those that a mesh axis runs over, the one named last changes fastest.
Arguments:
- features: bfloat16 [128, 4, 3072], P(('groups', 'rows')), parts along dimension 0, may hold values from -6 to 6
- cotangent: bfloat16 [128, 4, 3072], P(('groups', 'rows')), parts along dimension 0, may hold values from -6 to 6
- depth_kernel: float32 [7, 7, 3072], replicated, may hold values from -0.875 to 0.875
- depth_bias: float32 [3072], replicated, may hold values from -3 to 3
- norm_gain: float32 [3072], replicated, may hold values from 0.1 to 1.9
- norm_shift: float32 [3072], replicated, may hold values from -3 to 3
- up_weight: bfloat16 [3072, 12288], P(None, 'rows'), may hold values from -0.109375 to 0.109375
- up_bias: float32 [12288], P('rows'), may hold values from -3 to 3
- down_weight: bfloat16 [12288, 3072], P('rows'), may hold values from -0.109375 to 0.109375
- layer_scale: float32 [3072], replicated, may hold values from 0.3 to 3
Outputs:
- input_grad: bfloat16 [128, 4, 3072], P(('groups', 'rows')), parts along dimension 0
- up_grad: float32 [6144, 12288], P('groups', 'rows'), parts along dimension 0
- up_bias_grad: float32 [24576], P(('groups', 'rows')), parts along dimension 0
- down_grad: float32 [24576, 3072], P(('groups', 'rows')), parts along dimension 0
- kernel_grad: float32 [14, 7, 3072], P('groups'), parts along dimension 0
- depth_bias_grad: float32 [6144], P('groups'), parts along dimension 0
- gain_grad: float32 [6144], P('groups'), parts along dimension 0
- shift_grad: float32 [6144], P('groups'), parts along dimension 0
There are 2 independent parts, one for each index of `groups`. A program takes and returns all parts, laid end to end along the dimension named above; an argument that names none is the same for every part. Nothing has to cross between parts.
All inputs are finite; a program needn't handle non-finite values.
Results may differ from a plain program's by a relative error of at most 0.0075.
Values may be sent and summed in bfloat16 or wider, within the bound.
No kernel may reach another device: no remote copies, remote signals or barrier semaphores. Data moves between devices by JAX's collectives and lax.ppermute only.
A program may use at most 128 MiB of HBM per device.

v0:
```python
import jax
import jax.numpy as jnp
from jax import lax
from jax.sharding import PartitionSpec as P

IMG_ROWS = 32


def extended(cells, sides, width):
    for axis, dim in sides:
        count = lax.axis_size(axis)
        head = lax.slice_in_dim(cells, 0, width, axis=dim)
        tail = lax.slice_in_dim(cells, cells.shape[dim] - width, cells.shape[dim], axis=dim)
        cells = jnp.concatenate(
            [
                lax.ppermute(tail, axis, [(i, (i + 1) % count) for i in range(count)]),
                cells,
                lax.ppermute(head, axis, [((i + 1) % count, i) for i in range(count)]),
            ],
            axis=dim,
        )
    return cells


def gelu_value(pre_act):
    return 0.5 * pre_act * (1.0 + jax.scipy.special.erf(pre_act * 0.7071067811865476))


def gelu_slope(pre_act):
    cdf_part = 0.5 * (1.0 + jax.scipy.special.erf(pre_act * 0.7071067811865476))
    return cdf_part + pre_act * jnp.exp(-0.5 * pre_act * pre_act) * 0.3989422804014327


def contract(left, right, left_dim, right_dim):
    return lax.dot_general(
        left, right, (((left_dim,), (right_dim,)), ((), ())), preferred_element_type=jnp.float32
    )


def depthwise(padded, kernel, offset_term, row_count, col_count):
    summed = jnp.zeros(padded[..., 3 : 3 + row_count, 3 : 3 + col_count, :].shape, padded.dtype)
    for tap_row in range(7):
        for tap_col in range(7):
            summed = (
                summed
                + kernel[tap_row, tap_col]
                * padded[..., tap_row : tap_row + row_count, tap_col : tap_col + col_count, :]
            )
    return summed + offset_term


def depthwise_back(padded_grad, kernel, row_count, col_count):
    summed = jnp.zeros(
        padded_grad[..., 3 : 3 + row_count, 3 : 3 + col_count, :].shape, padded_grad.dtype
    )
    for tap_row in range(7):
        for tap_col in range(7):
            summed = (
                summed
                + kernel[tap_row, tap_col]
                * padded_grad[
                    ...,
                    6 - tap_row : 6 - tap_row + row_count,
                    6 - tap_col : 6 - tap_col + col_count,
                    :,
                ]
            )
    return summed


def normalize(conv_out):
    row_mean = jnp.mean(conv_out, axis=-1, keepdims=True)
    centred = conv_out - row_mean
    inv_std = lax.rsqrt(jnp.mean(centred * centred, axis=-1, keepdims=True) + 1e-06)
    return (centred * inv_std, inv_std)


def norm_back(norm_grad, unit_norm, inv_std, norm_gain):
    scaled = norm_grad * norm_gain
    return inv_std * (
        scaled
        - jnp.mean(scaled, axis=-1, keepdims=True)
        - unit_norm * jnp.mean(scaled * unit_norm, axis=-1, keepdims=True)
    )


def pad_columns(block):
    return jnp.pad(block, ((0, 0), (3, 3), (0, 0)))


def on_device(
    features,
    cotangent,
    depth_kernel,
    depth_bias,
    norm_gain,
    norm_shift,
    up_weight,
    up_bias,
    down_weight,
    layer_scale,
):
    rows_dev, col_count, channels = features.shape
    total_rows = rows_dev * lax.axis_size("rows")
    half_image = IMG_ROWS // 2
    my_index = lax.axis_index("rows")
    first_row = my_index * rows_dev
    row_offsets = first_row - 3 + jnp.arange(rows_dev + 6, dtype=jnp.int32)
    row_image = jnp.mod(row_offsets - half_image, total_rows) // IMG_ROWS
    own_image = jnp.mod(first_row - half_image, total_rows) // IMG_ROWS
    row_mask = (row_image == own_image).astype(jnp.float32)[:, None, None]
    cot_scaled = (
        (cotangent.astype(jnp.float32) * layer_scale)
        .astype(jnp.bfloat16)
        .reshape(rows_dev * col_count, channels)
    )
    cot_all = lax.all_gather(cot_scaled, "rows", axis=0, tiled=True)
    near_rows = extended(features, (("rows", 0),), 3)
    padded = pad_columns(near_rows.astype(jnp.float32) * row_mask)
    conv_out = depthwise(padded, depth_kernel, depth_bias, rows_dev, col_count)
    unit_norm, inv_std = normalize(conv_out)
    normed = (
        (unit_norm * norm_gain + norm_shift)
        .astype(jnp.bfloat16)
        .reshape(rows_dev * col_count, channels)
    )
    normed_all = lax.all_gather(normed, "rows", axis=0, tiled=True)
    pre_act = jnp.dot(normed_all, up_weight, preferred_element_type=jnp.float32) + up_bias
    hidden = gelu_value(pre_act).astype(jnp.bfloat16)
    down_grad = contract(hidden, cot_all, 0, 0)
    hid_grad = contract(cot_all, down_weight, 1, 1)
    act_grad = (hid_grad * gelu_slope(pre_act)).astype(jnp.bfloat16)
    up_bias_grad = jnp.sum(act_grad.astype(jnp.float32), axis=0)
    up_grad = contract(normed_all, act_grad, 0, 0)
    norm_grad = lax.psum_scatter(
        contract(act_grad, up_weight, 1, 1), "rows", scatter_dimension=0, tiled=True
    ).reshape(rows_dev, col_count, channels)
    gain_part = jnp.sum(norm_grad * unit_norm, axis=(0, 1))
    shift_part = jnp.sum(norm_grad, axis=(0, 1))
    conv_grad = norm_back(norm_grad, unit_norm, inv_std, norm_gain)
    bias_part = jnp.sum(conv_grad, axis=(0, 1))
    kernel_rows = []
    for tap_row in range(7):
        kernel_cols = []
        for tap_col in range(7):
            kernel_cols.append(
                jnp.sum(
                    conv_grad
                    * padded[tap_row : tap_row + rows_dev, tap_col : tap_col + col_count, :],
                    axis=(0, 1),
                )
            )
        kernel_rows.append(jnp.stack(kernel_cols))
    kernel_part = jnp.stack(kernel_rows)
    near_grad = extended(conv_grad.astype(jnp.bfloat16), (("rows", 0),), 3).astype(conv_grad.dtype)
    grad_padded = pad_columns(near_grad * row_mask)
    back_term = depthwise_back(grad_padded, depth_kernel, rows_dev, col_count)
    input_grad = (cotangent.astype(jnp.float32) + back_term).astype(jnp.bfloat16)
    gain_grad, shift_grad, kernel_grad, depth_bias_grad = lax.psum(
        (gain_part, shift_part, kernel_part, bias_part), "rows"
    )
    return (
        input_grad,
        up_grad,
        up_bias_grad,
        down_grad,
        kernel_grad,
        depth_bias_grad,
        gain_grad,
        shift_grad,
    )


def solution(mesh):
    in_specs = (
        P(("groups", "rows"), None, None),
        P(("groups", "rows"), None, None),
        P(),
        P(),
        P(),
        P(),
        P(None, "rows"),
        P("rows"),
        P("rows", None),
        P(),
    )
    out_specs = (
        P(("groups", "rows"), None, None),
        P("groups", "rows"),
        P(("groups", "rows")),
        P(("groups", "rows"), None),
        P("groups", None, None),
        P("groups"),
        P("groups"),
        P("groups"),
    )
    return jax.shard_map(
        on_device, mesh=mesh, in_specs=in_specs, out_specs=out_specs, check_vma=False
    )
```

profile of v0, /device:TPU:0, one launch (start us, length us, event | category | flops | bytes accessed | tf_op | source)
XLA Modules:
  0.0 296.4 jit_solution(8445374431140622717)
XLA Ops:
  8.7 5.1 %collective-permute-start.1 = (bf16[3,4,3072]{2,1,0:T(4,128)(2,1)S(1)}, bf16[3,4,3072]{2,1,0:T(4,128)(2,1)S(1)}, u32[]{:S(2)}, u32[]{:S(2)}) collective-permute-start(bf16[3,4,3072]{2,1,0:T(4,128)(2,1)S(1)} %get-tuple-element.121), channel_id=1, source_target_pairs={{1,0},{2,1},{3,2},{4,3},{5,4},{6,5},{7,6},{8,7},{9,8},{10,9},{11,1... | collective-permute-start | bytes 221192 | tf_op jit(solution)/shard_map/ppermute | solution.py:18
  13.8 1.7 fusion.105
  15.6 2.3 fusion.103
  18.1 2.8 fusion.104
  21.6 1.1 convert_multiply_fusion.1
  22.7 5.2 %fusion.102 = (f32[4,4]{1,0:T(4,128)S(1)}, f32[4,4,3072]{2,1,0:T(4,128)S(1)}) fusion(f32[3072]{0:T(1024)S(1)} %copy-done.85, f32[3072]{0:T(1024)S(1)} %bitcast.139, f32[3072]{0:T(1024)S(1)} %bitcast.141, f32[3072]{0:T(1024)S(1)} %bitcast.145, f32[10,4,3072]{2,1,0:T(4,128)S(1)} %convert_multiply_fusion.1, f32[3072]{0:T(1024)S(1)} %bitcast.147, ...), kind=kLoop, calls=%fused_computation.279 | loop fusion | flops 4866032 | bytes 2678848 | tf_op jit(solution)/shard_map/reduce_sum | solution.py:72
  30.3 37.9 %all-gather.5.cloned.1.call-done = bf16[256,3072]{1,0:T(8,128)(2,1)} async-done(((bf16[16,3072]{1,0:T(8,128)(2,1)}), bf16[256,3072]{1,0:T(8,128)(2,1)}) %all-gather.5.cloned.1.call-update) | async-done | bytes 1572880 | tf_op jit(solution)/shard_map/all_gather | solution.py:127
  68.2 4.2 %convolution_add_fusion = f32[256,768]{1,0:T(8,128)S(1)} fusion(bf16[256,3072]{1,0:T(8,128)(2,1)} %all-gather.5.cloned.1.call-done, bf16[3072,768]{1,0:T(8,128)(2,1)} %param.16, f32[768]{0:T(1024)S(1)} %copy-done.88), kind=kOutput, calls=%fused_computation.85 | convolution fusion | flops 1208156160 | bytes 7080960 | tf_op jit(solution)/shard_map/dot_general | solution.py:128
  72.4 37.2 %all-gather.3.cloned.1.call-done = bf16[256,3072]{1,0:T(8,128)(2,1)} async-done(((bf16[16,3072]{1,0:T(8,128)(2,1)}), bf16[256,3072]{1,0:T(8,128)(2,1)}) %all-gather.3.cloned.1.call-update) | async-done | bytes 1572880 | tf_op jit(solution)/shard_map/all_gather | solution.py:117
  109.7 5.0 %convert_reduce_fusion = (f32[768]{0:T(1024)}, bf16[256,768]{1,0:T(8,128)(2,1)S(1)}) fusion(f32[256,768]{1,0:T(8,128)S(1)} %convolution_add_fusion, bf16[256,3072]{1,0:T(8,128)(2,1)} %all-gather.3.cloned.1.call-done, bf16[768,3072]{1,0:T(8,128)(2,1)} %param.18), kind=kOutput, calls=%fused_computation.93 | convolution fusion | flops 1210318080 | bytes 7474176 | tf_op jit(solution)/shard_map/dot_general | solution.py:35
  114.6 5.4 %fusion.108 = f32[256,3072]{1,0:T(8,128)} fusion(bf16[256,768]{1,0:T(8,128)(2,1)S(1)} %get-tuple-element.123, bf16[3072,768]{1,0:T(8,128)(2,1)} %param.16), kind=kOutput, calls=%fused_computation.285 | convolution fusion | flops 1207959552 | bytes 8257536 | tf_op jit(solution)/shard_map/dot_general | solution.py:35
  120.3 1.2 copy-done
  121.5 5.2 %fusion.109 = f32[3072,768]{1,0:T(8,128)} fusion(bf16[256,3072]{1,0:T(8,128)(2,1)S(1)} %copy-done, bf16[256,768]{1,0:T(8,128)(2,1)S(1)} %get-tuple-element.123), kind=kOutput, calls=%fused_computation.286 | convolution fusion | flops 1207959552 | bytes 11403264 | tf_op jit(solution)/shard_map/dot_general | solution.py:35
  126.7 5.2 %fusion.5 = f32[768,3072]{1,0:T(8,128)} fusion(bf16[256,3072]{1,0:T(8,128)(2,1)S(1)} %copy-done.1, f32[256,768]{1,0:T(8,128)S(1)} %convolution_add_fusion), kind=kOutput, calls=%fused_computation.97 | convolution fusion | flops 1208942592 | bytes 11796480 | tf_op jit(solution)/shard_map/dot_general | solution.py:35
  131.9 53.5 %reduce-scatter.2.cloned.1.call-done = f32[16,3072]{1,0:T(8,128)} async-done(((f32[256,3072]{1,0:T(8,128)}), f32[16,3072]{1,0:T(8,128)}) %reduce-scatter.2.cloned.1.call-update) | async-done | bytes 196624 | tf_op jit(solution)/shard_map/reduce_scatter | solution.py:135
  185.4 1.1 fusion.101
  187.8 1.5 multiply_reduce_fusion.1
  189.3 1.0 multiply_reduce_fusion.37
  190.3 1.3 multiply_reduce_fusion.19
  191.8 4.4 %collective-permute-start.3 = (bf16[3,4,3072]{2,1,0:T(4,128)(2,1)S(1)}, bf16[3,4,3072]{2,1,0:T(4,128)(2,1)S(1)}, u32[]{:S(2)}, u32[]{:S(2)}) collective-permute-start(bf16[3,4,3072]{2,1,0:T(4,128)(2,1)S(1)} %get-tuple-element.119), channel_id=1, source_target_pairs={{1,0},{2,1},{3,2},{4,3},{5,4},{6,5},{7,6},{8,7},{9,8},{10,9},{11,1... | collective-permute-start | bytes 221192 | tf_op jit(solution)/shard_map/ppermute | solution.py:18
  198.6 58.5 %all-reduce.2 = (f32[3072]{0:T(1024)}, f32[3072]{0:T(1024)}, f32[3072]{0:T(1024)}) all-reduce(f32[3072]{0:T(1024)S(1)} %get-tuple-element.61, f32[3072]{0:T(1024)S(1)} %get-tuple-element.57, f32[3072]{0:T(1024)S(1)} %get-tuple-element.59), channel_id=1, replica_groups=mesh['groups'=2,'rows'=16] {'rows'}, use_global_device_ids=true, to_apply=%region_57.58 | all-reduce | flops 9216 | bytes 73728 | tf_op jit(solution)/shard_map/psum | solution.py:159
  258.3 4.2 %fusion.8 = bf16[4,4,3072]{2,1,0:T(4,128)(2,1)} fusion(bf16[4,4,3072]{2,1,0:T(4,128)(2,1)S(1)} %copy-done.3, f32[10,4,3072]{2,1,0:T(4,128)S(1)} %convert_multiply_fusion, f32[3072]{0:T(1024)S(1)} %bitcast.140, f32[3072]{0:T(1024)S(1)} %bitcast.142, f32[3072]{0:T(1024)S(1)} %bitcast.146, f32[3072]{0:T(1024)S(1)} %bitcast.148, f32[3072]{0:T(1024)S(1)} %bitcast.150, ...), kind=kLoop, calls=%fused_computation.102 | loop fusion | flops 4915200 | bytes 2666496 | tf_op jit(solution)/shard_map/convert_element_type | solution.py:158
  262.6 25.3 %all-reduce.5.cloned.1.call-done = f32[7,7,3072]{2,1,0:T(8,128)} async-done(((f32[7,7,3072]{2,1,0:T(8,128)}), f32[7,7,3072]{2,1,0:T(8,128)}) %all-reduce.5.cloned.1.call-update) | async-done | bytes 602128 | tf_op jit(solution)/shard_map/psum | solution.py:159
  287.9 2.0 copy.25
  (221 shorter events, 8.8 us)
Async XLA Ops:
  7.2 61.0 %all-gather.5.cloned.1.call-start = ((), (), s32[]{:S(2)}) async-start(), calls=%async_computation.2 | async-start | bytes 1671168 | tf_op jit(solution)/shard_map/all_gather | solution.py:127
  8.2 13.4 %collective-permute-start = (bf16[3,4,3072]{2,1,0:T(4,128)(2,1)S(1)}, bf16[3,4,3072]{2,1,0:T(4,128)(2,1)S(1)}, u32[]{:S(2)}, u32[]{:S(2)}) collective-permute-start(bf16[3,4,3072]{2,1,0:T(4,128)(2,1)S(1)} %get-tuple-element.120), channel_id=1, source_target_pairs={{0,1},{1,2},{2,3},{3,4},{4,5},{5,6},{6,7},{7,8},{8,9},{9,10},{10,1... | collective-permute-start | bytes 221192 | tf_op jit(solution)/shard_map/ppermute | solution.py:16
  8.7 12.9 %collective-permute-start.1 = (bf16[3,4,3072]{2,1,0:T(4,128)(2,1)S(1)}, bf16[3,4,3072]{2,1,0:T(4,128)(2,1)S(1)}, u32[]{:S(2)}, u32[]{:S(2)}) collective-permute-start(bf16[3,4,3072]{2,1,0:T(4,128)(2,1)S(1)} %get-tuple-element.121), channel_id=1, source_target_pairs={{1,0},{2,1},{3,2},{4,3},{5,4},{6,5},{7,6},{8,7},{9,8},{10,9},{11,1... | collective-permute-start | bytes 221192 | tf_op jit(solution)/shard_map/ppermute | solution.py:18
  29.5 80.2 %all-gather.3.cloned.1.call-start = ((), (), s32[]{:S(2)}) async-start(), calls=%async_computation.1 | async-start | bytes 1671168 | tf_op jit(solution)/shard_map/all_gather | solution.py:117
  30.3 155.1 %reduce-scatter.2.cloned.1.call-start = ((), (), s32[]{:S(2)}) async-start(), calls=%async_computation.3 | async-start | bytes 3342336 | tf_op jit(solution)/shard_map/reduce_scatter | solution.py:135
  120.1 167.8 %all-reduce.5.cloned.1.call-start = ((), (), s32[]{:S(2)}) async-start(), calls=%async_computation.4 | async-start | bytes 1376256 | tf_op jit(solution)/shard_map/psum | solution.py:159
  191.7 65.4 %collective-permute-start.2 = (bf16[3,4,3072]{2,1,0:T(4,128)(2,1)S(1)}, bf16[3,4,3072]{2,1,0:T(4,128)(2,1)S(1)}, u32[]{:S(2)}, u32[]{:S(2)}) collective-permute-start(bf16[3,4,3072]{2,1,0:T(4,128)(2,1)S(1)} %get-tuple-element.118), channel_id=1, source_target_pairs={{0,1},{1,2},{2,3},{3,4},{4,5},{5,6},{6,7},{7,8},{8,9},{9,10},{10,1... | collective-permute-start | bytes 221192 | tf_op jit(solution)/shard_map/ppermute | solution.py:16
  191.8 65.3 %collective-permute-start.3 = (bf16[3,4,3072]{2,1,0:T(4,128)(2,1)S(1)}, bf16[3,4,3072]{2,1,0:T(4,128)(2,1)S(1)}, u32[]{:S(2)}, u32[]{:S(2)}) collective-permute-start(bf16[3,4,3072]{2,1,0:T(4,128)(2,1)S(1)} %get-tuple-element.119), channel_id=1, source_target_pairs={{1,0},{2,1},{3,2},{4,3},{5,4},{6,5},{7,6},{8,7},{9,8},{10,9},{11,1... | collective-permute-start | bytes 221192 | tf_op jit(solution)/shard_map/ppermute | solution.py:18
  196.4 61.6 %copy-start.6 = (f32[1,1,3072]{2,1,0:T(1,128)S(1)}, f32[1,1,3072]{2,1,0:T(1,128)}, u32[]{:S(2)}) copy-start(f32[1,1,3072]{2,1,0:T(1,128)} %copy-done.5) | copy-start | bytes 36868
  196.4 61.6 %copy-start.8 = (f32[1,1,3072]{2,1,0:T(1,128)S(1)}, f32[1,1,3072]{2,1,0:T(1,128)}, u32[]{:S(2)}) copy-start(f32[1,1,3072]{2,1,0:T(1,128)} %copy-done.7) | copy-start | bytes 36868
  196.4 61.6 %copy-start.10 = (f32[1,1,3072]{2,1,0:T(1,128)S(1)}, f32[1,1,3072]{2,1,0:T(1,128)}, u32[]{:S(2)}) copy-start(f32[1,1,3072]{2,1,0:T(1,128)} %copy-done.9) | copy-start | bytes 36868
  196.4 61.6 %copy-start.12 = (f32[1,1,3072]{2,1,0:T(1,128)S(1)}, f32[1,1,3072]{2,1,0:T(1,128)}, u32[]{:S(2)}) copy-start(f32[1,1,3072]{2,1,0:T(1,128)} %copy-done.11) | copy-start | bytes 36868
  196.4 61.6 %copy-start.14 = (f32[1,1,3072]{2,1,0:T(1,128)S(1)}, f32[1,1,3072]{2,1,0:T(1,128)}, u32[]{:S(2)}) copy-start(f32[1,1,3072]{2,1,0:T(1,128)} %copy-done.13) | copy-start | bytes 36868
  196.4 61.6 %copy-start.16 = (f32[1,1,3072]{2,1,0:T(1,128)S(1)}, f32[1,1,3072]{2,1,0:T(1,128)}, u32[]{:S(2)}) copy-start(f32[1,1,3072]{2,1,0:T(1,128)} %copy-done.15) | copy-start | bytes 36868
  196.4 61.6 %copy-start.18 = (f32[1,1,3072]{2,1,0:T(1,128)S(1)}, f32[1,1,3072]{2,1,0:T(1,128)}, u32[]{:S(2)}) copy-start(f32[1,1,3072]{2,1,0:T(1,128)} %copy-done.17) | copy-start | bytes 36868
  196.4 61.6 %copy-start.20 = (f32[1,1,3072]{2,1,0:T(1,128)S(1)}, f32[1,1,3072]{2,1,0:T(1,128)}, u32[]{:S(2)}) copy-start(f32[1,1,3072]{2,1,0:T(1,128)} %copy-done.19) | copy-start | bytes 36868
  196.4 61.6 %copy-start.22 = (f32[1,1,3072]{2,1,0:T(1,128)S(1)}, f32[1,1,3072]{2,1,0:T(1,128)}, u32[]{:S(2)}) copy-start(f32[1,1,3072]{2,1,0:T(1,128)} %copy-done.21) | copy-start | bytes 36868
  196.4 61.6 %copy-start.24 = (f32[1,1,3072]{2,1,0:T(1,128)S(1)}, f32[1,1,3072]{2,1,0:T(1,128)}, u32[]{:S(2)}) copy-start(f32[1,1,3072]{2,1,0:T(1,128)} %copy-done.23) | copy-start | bytes 36868
  196.5 61.6 %copy-start.26 = (f32[1,1,3072]{2,1,0:T(1,128)S(1)}, f32[1,1,3072]{2,1,0:T(1,128)}, u32[]{:S(2)}) copy-start(f32[1,1,3072]{2,1,0:T(1,128)} %copy-done.25) | copy-start | bytes 36868
  196.5 61.6 %copy-start.28 = (f32[1,1,3072]{2,1,0:T(1,128)S(1)}, f32[1,1,3072]{2,1,0:T(1,128)}, u32[]{:S(2)}) copy-start(f32[1,1,3072]{2,1,0:T(1,128)} %copy-done.27) | copy-start | bytes 36868
  196.5 61.6 %copy-start.30 = (f32[1,1,3072]{2,1,0:T(1,128)S(1)}, f32[1,1,3072]{2,1,0:T(1,128)}, u32[]{:S(2)}) copy-start(f32[1,1,3072]{2,1,0:T(1,128)} %copy-done.29) | copy-start | bytes 36868
  196.5 61.6 %copy-start.32 = (f32[1,1,3072]{2,1,0:T(1,128)S(1)}, f32[1,1,3072]{2,1,0:T(1,128)}, u32[]{:S(2)}) copy-start(f32[1,1,3072]{2,1,0:T(1,128)} %copy-done.31) | copy-start | bytes 36868
  196.5 61.6 %copy-start.34 = (f32[1,1,3072]{2,1,0:T(1,128)S(1)}, f32[1,1,3072]{2,1,0:T(1,128)}, u32[]{:S(2)}) copy-start(f32[1,1,3072]{2,1,0:T(1,128)} %copy-done.33) | copy-start | bytes 36868
  196.5 61.6 %copy-start.36 = (f32[1,1,3072]{2,1,0:T(1,128)S(1)}, f32[1,1,3072]{2,1,0:T(1,128)}, u32[]{:S(2)}) copy-start(f32[1,1,3072]{2,1,0:T(1,128)} %copy-done.35) | copy-start | bytes 36868
  (73 other events, 1978.4 us)
Sparse Core Ops, SparseCore 0:
  29.6 38.5 all-gather.4
  71.1 38.5 all-gather.2
  120.2 65.0 reduce-scatter.1
  198.7 89.1 all-reduce.4
where the time goes:
time: 297 us; the launch traced here: 296 us
  waiting for transfers between devices  154 us (52%)
  blocking collectives  58.5 us (20%)
  matrix products  25 us (8%)
  other arithmetic  17.7 us (6%)
  local copies, waits for them, and re-layouts  15.6 us (5%)
  between operations  15.3 us (5%)
  starting transfers between devices  10.4 us (4%)
    psum x1, blocking collectives, on_device(): lax.psum((gain_part, shift_part, kernel_part, bias_part), 'rows')  58.5 us
    reduce_scatter x1, waiting for transfers between devices, on_device(): lax.psum_scatter(contract(act_grad, up_weight, 1, 1), 'rows', scatter_dim...  53.5 us
    all_gather x1, waiting for transfers between devices, on_device(): normed_all = lax.all_gather(normed, 'rows', axis=0, tiled=True)  37.9 us
    all_gather x1, waiting for transfers between devices, on_device(): cot_all = lax.all_gather(cot_scaled, 'rows', axis=0, tiled=True)  37.2 us
    psum x1, waiting for transfers between devices, on_device(): lax.psum((gain_part, shift_part, kernel_part, bias_part), 'rows')  25.3 us
    dot_general x4, matrix products, contract(): lax.dot_general(left, right, (((left_dim,), (right_dim,)), ((), ())), pre...  20.8 us
    ppermute x2, starting transfers between devices, extended(): lax.ppermute(head, axis, [((i + 1) % count, i) for i in range(count)])  9.49 us
  transfers between devices with their start and end apart: 8, of which 4 were waited for; matrix products, arithmetic and copies ran while one was open for 10% of the time, Pallas kernels for 0%

commit v1 on v0

--- a/solution.py
+++ b/solution.py
@@ -114,7 +114,24 @@
         .astype(jnp.bfloat16)
         .reshape(rows_dev * col_count, channels)
     )
-    cot_all = lax.all_gather(cot_scaled, "rows", axis=0, tiled=True)
+    ways, here, step = (lax.axis_size("rows"), lax.axis_index("rows"), cot_scaled.shape[0])
+    shape = [n * ways if d == 0 else n for d, n in enumerate(cot_scaled.shape)]
+    cot_all = lax.dynamic_update_slice_in_dim(
+        jnp.zeros(shape, cot_scaled.dtype), cot_scaled, here * step, axis=0
+    )
+    going_up = going_down = cot_scaled
+    for far in range(1, ways // 2 + 1):
+        going_up = lax.ppermute(going_up, "rows", [(d, (d + 1) % ways) for d in range(ways)])
+        cot_all = lax.dynamic_update_slice_in_dim(
+            cot_all, going_up, (here - far) % ways * step, axis=0
+        )
+        if 2 * far < ways:
+            going_down = lax.ppermute(
+                going_down, "rows", [(d, (d - 1) % ways) for d in range(ways)]
+            )
+            cot_all = lax.dynamic_update_slice_in_dim(
+                cot_all, going_down, (here + far) % ways * step, axis=0
+            )
     near_rows = extended(features, (("rows", 0),), 3)
     padded = pad_columns(near_rows.astype(jnp.float32) * row_mask)
     conv_out = depthwise(padded, depth_kernel, depth_bias, rows_dev, col_count)

time: 297 us -> 272 us (0.916)
  waiting for transfers between devices: 154 us -> 105 us
  starting transfers between devices: 10.4 us -> 40.6 us
  local copies, waits for them, and re-layouts: 15.6 us -> 10 us
    all_gather x1, waiting for transfers between devices: 37.9 us -> 0.02 us  [on_device(): normed_all = lax.all_gather(normed, 'rows', axis=0, tiled=True)]
    all_gather x1 -> x0, waiting for transfers between devices: 37.2 us -> none  [on_device(): cot_all = lax.all_gather(cot_scaled, 'rows', axis=0, tiled=True)]
    ppermute x0 -> x15, starting transfers between devices: none -> 31.2 us  [the longest x7 31.2 us: on_device(): lax.ppermute(going_down, 'rows', [(d, (d - 1) % ways) for d in range(ways)])]
    ppermute x0 -> x15, waiting for transfers between devices: none -> 26.7 us  [the longest x8 17.9 us: on_device(): lax.ppermute(going_up, 'rows', [(d, (d + 1) % ways) for d in range(ways)])]
  transfers between devices with their start and end apart: 8 -> 22, of which waited for: 4 -> 13; matrix products, arithmetic and copies ran while one was open for 10% -> 11% of each run, Pallas kernels for 0% -> 0%
where the time goes in v1:
time: 272 us; the launch traced here: 271 us
  waiting for transfers between devices  105 us (39%)
  blocking collectives  58.5 us (22%)
  starting transfers between devices  40.6 us (15%)
  matrix products  23.8 us (9%)
  other arithmetic  17.9 us (7%)
  between operations  15.5 us (6%)
  local copies, waits for them, and re-layouts  10 us (4%)
    psum x1, blocking collectives, on_device(): lax.psum((gain_part, shift_part, kernel_part, bias_part), 'rows')  58.5 us
    reduce_scatter x1, waiting for transfers between devices, on_device(): lax.psum_scatter(contract(act_grad, up_weight, 1, 1), 'rows', scatter_dim...  52.4 us
    ppermute x7, starting transfers between devices, on_device(): lax.ppermute(going_down, 'rows', [(d, (d - 1) % ways) for d in range(ways)])  31.2 us
    psum x1, waiting for transfers between devices, on_device(): lax.psum((gain_part, shift_part, kernel_part, bias_part), 'rows')  25.6 us
    dot_general x4, matrix products, contract(): lax.dot_general(left, right, (((left_dim,), (right_dim,)), ((), ())), pre...  19.4 us
    ppermute x8, waiting for transfers between devices, on_device(): lax.ppermute(going_up, 'rows', [(d, (d + 1) % ways) for d in range(ways)])  17.9 us
    ppermute x2, starting transfers between devices, extended(): lax.ppermute(head, axis, [((i + 1) % count, i) for i in range(count)])  8.92 us
    ppermute x7, waiting for transfers between devices, on_device(): lax.ppermute(going_down, 'rows', [(d, (d - 1) % ways) for d in range(ways)])  8.75 us
  transfers between devices with their start and end apart: 22, of which 13 were waited for; matrix products, arithmetic and copies ran while one was open for 11% of the time, Pallas kernels for 0%

profile of v1, /device:TPU:0, one launch (start us, length us, event | category | flops | bytes accessed | tf_op | source)
XLA Modules:
  0.0 271.1 jit_solution(14453638341192140194)
XLA Ops:
  8.3 5.5 %collective-permute-start.3 = (bf16[16,3072]{1,0:T(8,128)(2,1)S(1)}, bf16[16,3072]{1,0:T(8,128)(2,1)S(1)}, u32[]{:S(2)}, u32[]{:S(2)}) collective-permute-start(bf16[16,3072]{1,0:T(8,128)(2,1)S(1)} %reshape.89), channel_id=1, source_target_pairs={{0,15},{1,0},{2,1},{3,2},{4,3},{5,4},{6,5},{7,6},{8,7},{9,8},{10,9... | collective-permute-start | bytes 294920 | tf_op jit(solution)/shard_map/ppermute | solution.py:129
  14.8 4.5 %collective-permute-start.1 = (bf16[3,4,3072]{2,1,0:T(4,128)(2,1)S(1)}, bf16[3,4,3072]{2,1,0:T(4,128)(2,1)S(1)}, u32[]{:S(2)}, u32[]{:S(2)}) collective-permute-start(bf16[3,4,3072]{2,1,0:T(4,128)(2,1)S(1)} %get-tuple-element.121), channel_id=1, source_target_pairs={{1,0},{2,1},{3,2},{4,3},{5,4},{6,5},{7,6},{8,7},{9,8},{10,9},{11,1... | collective-permute-start | bytes 221192 | tf_op jit(solution)/shard_map/ppermute | solution.py:18
  24.2 5.1 %fusion.102 = (f32[4,4]{1,0:T(4,128)S(1)}, f32[4,4,3072]{2,1,0:T(4,128)S(1)}) fusion(f32[3072]{0:T(1024)S(1)} %copy-done.85, f32[3072]{0:T(1024)S(1)} %bitcast.141, f32[3072]{0:T(1024)S(1)} %bitcast.143, f32[3072]{0:T(1024)S(1)} %bitcast.147, f32[10,4,3072]{2,1,0:T(4,128)S(1)} %convert_multiply_fusion.1, f32[3072]{0:T(1024)S(1)} %bitcast.149, ...), kind=kLoop, calls=%fused_computation.295 | loop fusion | flops 4866032 | bytes 2678848 | tf_op jit(solution)/shard_map/reduce_sum | solution.py:72
  30.7 2.7 collective-permute-start.5
  33.4 2.2 collective-permute-done.5
  35.5 4.6 %collective-permute-start.7 = (bf16[16,3072]{1,0:T(8,128)(2,1)S(1)}, bf16[16,3072]{1,0:T(8,128)(2,1)S(1)}, u32[]{:S(2)}, u32[]{:S(2)}) collective-permute-start(bf16[16,3072]{1,0:T(8,128)(2,1)S(1)} %collective-permute-done.5), channel_id=1, source_target_pairs={{0,15},{1,0},{2,1},{3,2},{4,3},{5,4},{6,5},{7,6},{8,7},{9,8},{10,9... | collective-permute-start | bytes 294920 | tf_op jit(solution)/shard_map/ppermute | solution.py:129
  40.2 2.2 collective-permute-done.7
  42.4 4.6 %collective-permute-start.9 = (bf16[16,3072]{1,0:T(8,128)(2,1)S(1)}, bf16[16,3072]{1,0:T(8,128)(2,1)S(1)}, u32[]{:S(2)}, u32[]{:S(2)}) collective-permute-start(bf16[16,3072]{1,0:T(8,128)(2,1)S(1)} %collective-permute-done.7), channel_id=1, source_target_pairs={{0,15},{1,0},{2,1},{3,2},{4,3},{5,4},{6,5},{7,6},{8,7},{9,8},{10,9... | collective-permute-start | bytes 294920 | tf_op jit(solution)/shard_map/ppermute | solution.py:129
  49.4 4.6 %collective-permute-start.11 = (bf16[16,3072]{1,0:T(8,128)(2,1)S(1)}, bf16[16,3072]{1,0:T(8,128)(2,1)S(1)}, u32[]{:S(2)}, u32[]{:S(2)}) collective-permute-start(bf16[16,3072]{1,0:T(8,128)(2,1)S(1)} %collective-permute-done.9), channel_id=1, source_target_pairs={{0,15},{1,0},{2,1},{3,2},{4,3},{5,4},{6,5},{7,6},{8,7},{9,8},{10,9... | collective-permute-start | bytes 294920 | tf_op jit(solution)/shard_map/ppermute | solution.py:129
  56.2 4.6 %collective-permute-start.13 = (bf16[16,3072]{1,0:T(8,128)(2,1)S(1)}, bf16[16,3072]{1,0:T(8,128)(2,1)S(1)}, u32[]{:S(2)}, u32[]{:S(2)}) collective-permute-start(bf16[16,3072]{1,0:T(8,128)(2,1)S(1)} %collective-permute-done.11), channel_id=1, source_target_pairs={{0,15},{1,0},{2,1},{3,2},{4,3},{5,4},{6,5},{7,6},{8,7},{9,8},{10,9... | collective-permute-start | bytes 294920 | tf_op jit(solution)/shard_map/ppermute | solution.py:129
  63.0 4.6 %collective-permute-start.15 = (bf16[16,3072]{1,0:T(8,128)(2,1)S(1)}, bf16[16,3072]{1,0:T(8,128)(2,1)S(1)}, u32[]{:S(2)}, u32[]{:S(2)}) collective-permute-start(bf16[16,3072]{1,0:T(8,128)(2,1)S(1)} %collective-permute-done.13), channel_id=1, source_target_pairs={{0,15},{1,0},{2,1},{3,2},{4,3},{5,4},{6,5},{7,6},{8,7},{9,8},{10,9... | collective-permute-start | bytes 294920 | tf_op jit(solution)/shard_map/ppermute | solution.py:129
  67.6 2.3 collective-permute-done.12
  69.9 6.7 %collective-permute-done.14 = bf16[16,3072]{1,0:T(8,128)(2,1)S(1)} collective-permute-done((bf16[16,3072]{1,0:T(8,128)(2,1)S(1)}, bf16[16,3072]{1,0:T(8,128)(2,1)S(1)}, u32[]{:S(2)}, u32[]{:S(2)}) %collective-permute-start.14) | collective-permute-done | bytes 98336 | tf_op jit(solution)/shard_map/ppermute | solution.py:124
  76.7 6.7 %collective-permute-done.16 = bf16[16,3072]{1,0:T(8,128)(2,1)S(1)} collective-permute-done((bf16[16,3072]{1,0:T(8,128)(2,1)S(1)}, bf16[16,3072]{1,0:T(8,128)(2,1)S(1)}, u32[]{:S(2)}, u32[]{:S(2)}) %collective-permute-start.16) | collective-permute-done | bytes 98336 | tf_op jit(solution)/shard_map/ppermute | solution.py:124
  83.4 4.3 %convolution_add_fusion = f32[256,768]{1,0:T(8,128)S(1)} fusion(bf16[256,3072]{1,0:T(8,128)(2,1)} %all-gather.2.cloned.1.call-done, bf16[3072,768]{1,0:T(8,128)(2,1)} %param.16, f32[768]{0:T(1024)S(1)} %copy-done.87), kind=kOutput, calls=%fused_computation.85 | convolution fusion | flops 1208156160 | bytes 7080960 | tf_op jit(solution)/shard_map/dot_general | solution.py:145
  87.8 4.6 %convert_reduce_fusion = (f32[768]{0:T(1024)}, bf16[256,768]{1,0:T(8,128)(2,1)S(1)}) fusion(f32[256,768]{1,0:T(8,128)S(1)} %convolution_add_fusion, bf16[256,3072]{1,0:T(8,128)(2,1)S(1)} %constant_dynamic-update-slice_fusion, bf16[768,3072]{1,0:T(8,128)(2,1)} %param.18), kind=kOutput, calls=%fused_computation.93 | convolution fusion | flops 1210318080 | bytes 7474176 | tf_op jit(solution)/shard_map/dot_general | solution.py:35
  92.4 3.1 %fusion.108 = f32[256,3072]{1,0:T(8,128)} fusion(bf16[256,768]{1,0:T(8,128)(2,1)S(1)} %get-tuple-element.123, bf16[3072,768]{1,0:T(8,128)(2,1)S(1)} %bitcast.122), kind=kOutput, calls=%fused_computation.301 | convolution fusion | flops 1207959552 | bytes 8257536 | tf_op jit(solution)/shard_map/dot_general | solution.py:35
  95.7 6.6 %fusion.109 = f32[3072,768]{1,0:T(8,128)} fusion(bf16[256,3072]{1,0:T(8,128)(2,1)} %all-gather.2.cloned.1.call-done, bf16[256,768]{1,0:T(8,128)(2,1)S(1)} %get-tuple-element.123), kind=kOutput, calls=%fused_computation.302 | convolution fusion | flops 1207959552 | bytes 11403264 | tf_op jit(solution)/shard_map/dot_general | solution.py:35
  102.3 5.2 %fusion.5 = f32[768,3072]{1,0:T(8,128)} fusion(bf16[256,3072]{1,0:T(8,128)(2,1)S(1)} %constant_dynamic-update-slice_fusion, f32[256,768]{1,0:T(8,128)S(1)} %convolution_add_fusion), kind=kOutput, calls=%fused_computation.97 | convolution fusion | flops 1208942592 | bytes 11796480 | tf_op jit(solution)/shard_map/dot_general | solution.py:35
  107.5 52.4 %reduce-scatter.2.cloned.1.call-done = f32[16,3072]{1,0:T(8,128)} async-done(((f32[256,3072]{1,0:T(8,128)}), f32[16,3072]{1,0:T(8,128)}) %reduce-scatter.2.cloned.1.call-update) | async-done | bytes 196624 | tf_op jit(solution)/shard_map/reduce_scatter | solution.py:152
  166.3 4.4 %collective-permute-start.18 = (bf16[3,4,3072]{2,1,0:T(4,128)(2,1)S(1)}, bf16[3,4,3072]{2,1,0:T(4,128)(2,1)S(1)}, u32[]{:S(2)}, u32[]{:S(2)}) collective-permute-start(bf16[3,4,3072]{2,1,0:T(4,128)(2,1)S(1)} %get-tuple-element.119), channel_id=1, source_target_pairs={{1,0},{2,1},{3,2},{4,3},{5,4},{6,5},{7,6},{8,7},{9,8},{10,9},{11,1... | collective-permute-start | bytes 221192 | tf_op jit(solution)/shard_map/ppermute | solution.py:18
  173.1 58.5 %all-reduce.2 = (f32[3072]{0:T(1024)}, f32[3072]{0:T(1024)}, f32[3072]{0:T(1024)}) all-reduce(f32[3072]{0:T(1024)S(1)} %get-tuple-element.61, f32[3072]{0:T(1024)S(1)} %get-tuple-element.57, f32[3072]{0:T(1024)S(1)} %get-tuple-element.59), channel_id=1, replica_groups=mesh['groups'=2,'rows'=16] {'rows'}, use_global_device_ids=true, to_apply=%region_57.58 | all-reduce | flops 9216 | bytes 73728 | tf_op jit(solution)/shard_map/psum | solution.py:176
  232.9 4.1 %fusion.8 = bf16[4,4,3072]{2,1,0:T(4,128)(2,1)} fusion(bf16[4,4,3072]{2,1,0:T(4,128)(2,1)S(1)} %copy-done.3, f32[10,4,3072]{2,1,0:T(4,128)S(1)} %convert_multiply_fusion, f32[3072]{0:T(1024)S(1)} %bitcast.142, f32[3072]{0:T(1024)S(1)} %bitcast.144, f32[3072]{0:T(1024)S(1)} %bitcast.148, f32[3072]{0:T(1024)S(1)} %bitcast.150, f32[3072]{0:T(1024)S(1)} %bitcast.152, ...), kind=kLoop, calls=%fused_computation.102 | loop fusion | flops 4915200 | bytes 2666496 | tf_op jit(solution)/shard_map/convert_element_type | solution.py:175
  237.0 25.6 %all-reduce.5.cloned.1.call-done = f32[7,7,3072]{2,1,0:T(8,128)} async-done(((f32[7,7,3072]{2,1,0:T(8,128)}), f32[7,7,3072]{2,1,0:T(8,128)}) %all-reduce.5.cloned.1.call-update) | async-done | bytes 602128 | tf_op jit(solution)/shard_map/psum | solution.py:176
  (268 shorter events, 25.9 us)
Async XLA Ops:
  7.2 76.2 %all-gather.2.cloned.1.call-start = ((), (), s32[]{:S(2)}) async-start(), calls=%async_computation.1 | async-start | bytes 1671168 | tf_op jit(solution)/shard_map/all_gather | solution.py:144
  8.3 22.4 %collective-permute-start.3 = (bf16[16,3072]{1,0:T(8,128)(2,1)S(1)}, bf16[16,3072]{1,0:T(8,128)(2,1)S(1)}, u32[]{:S(2)}, u32[]{:S(2)}) collective-permute-start(bf16[16,3072]{1,0:T(8,128)(2,1)S(1)} %reshape.89), channel_id=1, source_target_pairs={{0,15},{1,0},{2,1},{3,2},{4,3},{5,4},{6,5},{7,6},{8,7},{9,8},{10,9... | collective-permute-start | bytes 294920 | tf_op jit(solution)/shard_map/ppermute | solution.py:129
  13.8 19.6 %collective-permute-start.2 = (bf16[16,3072]{1,0:T(8,128)(2,1)S(1)}, bf16[16,3072]{1,0:T(8,128)(2,1)S(1)}, u32[]{:S(2)}, u32[]{:S(2)}) collective-permute-start(bf16[16,3072]{1,0:T(8,128)(2,1)S(1)} %reshape.89), channel_id=1, source_target_pairs={{0,1},{1,2},{2,3},{3,4},{4,5},{5,6},{6,7},{7,8},{8,9},{9,10},{10,1... | collective-permute-start | bytes 294920 | tf_op jit(solution)/shard_map/ppermute | solution.py:124
  14.8 8.4 %collective-permute-start = (bf16[3,4,3072]{2,1,0:T(4,128)(2,1)S(1)}, bf16[3,4,3072]{2,1,0:T(4,128)(2,1)S(1)}, u32[]{:S(2)}, u32[]{:S(2)}) collective-permute-start(bf16[3,4,3072]{2,1,0:T(4,128)(2,1)S(1)} %get-tuple-element.120), channel_id=1, source_target_pairs={{0,1},{1,2},{2,3},{3,4},{4,5},{5,6},{6,7},{7,8},{8,9},{9,10},{10,1... | collective-permute-start | bytes 221192 | tf_op jit(solution)/shard_map/ppermute | solution.py:16
  14.8 8.3 %collective-permute-start.1 = (bf16[3,4,3072]{2,1,0:T(4,128)(2,1)S(1)}, bf16[3,4,3072]{2,1,0:T(4,128)(2,1)S(1)}, u32[]{:S(2)}, u32[]{:S(2)}) collective-permute-start(bf16[3,4,3072]{2,1,0:T(4,128)(2,1)S(1)} %get-tuple-element.121), channel_id=1, source_target_pairs={{1,0},{2,1},{3,2},{4,3},{5,4},{6,5},{7,6},{8,7},{9,8},{10,9},{11,1... | collective-permute-start | bytes 221192 | tf_op jit(solution)/shard_map/ppermute | solution.py:18
  30.6 129.3 %reduce-scatter.2.cloned.1.call-start = ((), (), s32[]{:S(2)}) async-start(), calls=%async_computation.2 | async-start | bytes 3342336 | tf_op jit(solution)/shard_map/reduce_scatter | solution.py:152
  30.7 4.9 %collective-permute-start.5 = (bf16[16,3072]{1,0:T(8,128)(2,1)S(1)}, bf16[16,3072]{1,0:T(8,128)(2,1)S(1)}, u32[]{:S(2)}, u32[]{:S(2)}) collective-permute-start(bf16[16,3072]{1,0:T(8,128)(2,1)S(1)} %collective-permute-done.3), channel_id=1, source_target_pairs={{0,15},{1,0},{2,1},{3,2},{4,3},{5,4},{6,5},{7,6},{8,7},{9,8},{10,9... | collective-permute-start | bytes 294920 | tf_op jit(solution)/shard_map/ppermute | solution.py:129
  33.3 6.8 %collective-permute-start.4 = (bf16[16,3072]{1,0:T(8,128)(2,1)S(1)}, bf16[16,3072]{1,0:T(8,128)(2,1)S(1)}, u32[]{:S(2)}, u32[]{:S(2)}) collective-permute-start(bf16[16,3072]{1,0:T(8,128)(2,1)S(1)} %collective-permute-done.2), channel_id=1, source_target_pairs={{0,1},{1,2},{2,3},{3,4},{4,5},{5,6},{6,7},{7,8},{8,9},{9,10},{10,1... | collective-permute-start | bytes 294920 | tf_op jit(solution)/shard_map/ppermute | solution.py:124
  35.5 6.8 %collective-permute-start.7 = (bf16[16,3072]{1,0:T(8,128)(2,1)S(1)}, bf16[16,3072]{1,0:T(8,128)(2,1)S(1)}, u32[]{:S(2)}, u32[]{:S(2)}) collective-permute-start(bf16[16,3072]{1,0:T(8,128)(2,1)S(1)} %collective-permute-done.5), channel_id=1, source_target_pairs={{0,15},{1,0},{2,1},{3,2},{4,3},{5,4},{6,5},{7,6},{8,7},{9,8},{10,9... | collective-permute-start | bytes 294920 | tf_op jit(solution)/shard_map/ppermute | solution.py:129
  40.2 7.6 %collective-permute-start.6 = (bf16[16,3072]{1,0:T(8,128)(2,1)S(1)}, bf16[16,3072]{1,0:T(8,128)(2,1)S(1)}, u32[]{:S(2)}, u32[]{:S(2)}) collective-permute-start(bf16[16,3072]{1,0:T(8,128)(2,1)S(1)} %collective-permute-done.4), channel_id=1, source_target_pairs={{0,1},{1,2},{2,3},{3,4},{4,5},{5,6},{6,7},{7,8},{8,9},{9,10},{10,1... | collective-permute-start | bytes 294920 | tf_op jit(solution)/shard_map/ppermute | solution.py:124
  42.4 7.0 %collective-permute-start.9 = (bf16[16,3072]{1,0:T(8,128)(2,1)S(1)}, bf16[16,3072]{1,0:T(8,128)(2,1)S(1)}, u32[]{:S(2)}, u32[]{:S(2)}) collective-permute-start(bf16[16,3072]{1,0:T(8,128)(2,1)S(1)} %collective-permute-done.7), channel_id=1, source_target_pairs={{0,15},{1,0},{2,1},{3,2},{4,3},{5,4},{6,5},{7,6},{8,7},{9,8},{10,9... | collective-permute-start | bytes 294920 | tf_op jit(solution)/shard_map/ppermute | solution.py:129
  47.7 6.8 %collective-permute-start.8 = (bf16[16,3072]{1,0:T(8,128)(2,1)S(1)}, bf16[16,3072]{1,0:T(8,128)(2,1)S(1)}, u32[]{:S(2)}, u32[]{:S(2)}) collective-permute-start(bf16[16,3072]{1,0:T(8,128)(2,1)S(1)} %collective-permute-done.6), channel_id=1, source_target_pairs={{0,1},{1,2},{2,3},{3,4},{4,5},{5,6},{6,7},{7,8},{8,9},{9,10},{10,1... | collective-permute-start | bytes 294920 | tf_op jit(solution)/shard_map/ppermute | solution.py:124
  49.4 6.8 %collective-permute-start.11 = (bf16[16,3072]{1,0:T(8,128)(2,1)S(1)}, bf16[16,3072]{1,0:T(8,128)(2,1)S(1)}, u32[]{:S(2)}, u32[]{:S(2)}) collective-permute-start(bf16[16,3072]{1,0:T(8,128)(2,1)S(1)} %collective-permute-done.9), channel_id=1, source_target_pairs={{0,15},{1,0},{2,1},{3,2},{4,3},{5,4},{6,5},{7,6},{8,7},{9,8},{10,9... | collective-permute-start | bytes 294920 | tf_op jit(solution)/shard_map/ppermute | solution.py:129
  54.5 7.4 %collective-permute-start.10 = (bf16[16,3072]{1,0:T(8,128)(2,1)S(1)}, bf16[16,3072]{1,0:T(8,128)(2,1)S(1)}, u32[]{:S(2)}, u32[]{:S(2)}) collective-permute-start(bf16[16,3072]{1,0:T(8,128)(2,1)S(1)} %collective-permute-done.8), channel_id=1, source_target_pairs={{0,1},{1,2},{2,3},{3,4},{4,5},{5,6},{6,7},{7,8},{8,9},{9,10},{10,1... | collective-permute-start | bytes 294920 | tf_op jit(solution)/shard_map/ppermute | solution.py:124
  56.2 6.8 %collective-permute-start.13 = (bf16[16,3072]{1,0:T(8,128)(2,1)S(1)}, bf16[16,3072]{1,0:T(8,128)(2,1)S(1)}, u32[]{:S(2)}, u32[]{:S(2)}) collective-permute-start(bf16[16,3072]{1,0:T(8,128)(2,1)S(1)} %collective-permute-done.11), channel_id=1, source_target_pairs={{0,15},{1,0},{2,1},{3,2},{4,3},{5,4},{6,5},{7,6},{8,7},{9,8},{10,9... | collective-permute-start | bytes 294920 | tf_op jit(solution)/shard_map/ppermute | solution.py:129
  61.9 8.0 %collective-permute-start.12 = (bf16[16,3072]{1,0:T(8,128)(2,1)S(1)}, bf16[16,3072]{1,0:T(8,128)(2,1)S(1)}, u32[]{:S(2)}, u32[]{:S(2)}) collective-permute-start(bf16[16,3072]{1,0:T(8,128)(2,1)S(1)} %collective-permute-done.10), channel_id=1, source_target_pairs={{0,1},{1,2},{2,3},{3,4},{4,5},{5,6},{6,7},{7,8},{8,9},{9,10},{10,1... | collective-permute-start | bytes 294920 | tf_op jit(solution)/shard_map/ppermute | solution.py:124
  63.0 13.6 %collective-permute-start.15 = (bf16[16,3072]{1,0:T(8,128)(2,1)S(1)}, bf16[16,3072]{1,0:T(8,128)(2,1)S(1)}, u32[]{:S(2)}, u32[]{:S(2)}) collective-permute-start(bf16[16,3072]{1,0:T(8,128)(2,1)S(1)} %collective-permute-done.13), channel_id=1, source_target_pairs={{0,15},{1,0},{2,1},{3,2},{4,3},{5,4},{6,5},{7,6},{8,7},{9,8},{10,9... | collective-permute-start | bytes 294920 | tf_op jit(solution)/shard_map/ppermute | solution.py:129
  69.9 6.7 %collective-permute-start.14 = (bf16[16,3072]{1,0:T(8,128)(2,1)S(1)}, bf16[16,3072]{1,0:T(8,128)(2,1)S(1)}, u32[]{:S(2)}, u32[]{:S(2)}) collective-permute-start(bf16[16,3072]{1,0:T(8,128)(2,1)S(1)} %collective-permute-done.12), channel_id=1, source_target_pairs={{0,1},{1,2},{2,3},{3,4},{4,5},{5,6},{6,7},{7,8},{8,9},{9,10},{10,1... | collective-permute-start | bytes 294920 | tf_op jit(solution)/shard_map/ppermute | solution.py:124
  76.6 6.7 %collective-permute-start.16 = (bf16[16,3072]{1,0:T(8,128)(2,1)S(1)}, bf16[16,3072]{1,0:T(8,128)(2,1)S(1)}, u32[]{:S(2)}, u32[]{:S(2)}) collective-permute-start(bf16[16,3072]{1,0:T(8,128)(2,1)S(1)} %collective-permute-done.14), channel_id=1, source_target_pairs={{0,1},{1,2},{2,3},{3,4},{4,5},{5,6},{6,7},{7,8},{8,9},{9,10},{10,1... | collective-permute-start | bytes 294920 | tf_op jit(solution)/shard_map/ppermute | solution.py:124
  95.5 167.1 %all-reduce.5.cloned.1.call-start = ((), (), s32[]{:S(2)}) async-start(), calls=%async_computation.3 | async-start | bytes 1376256 | tf_op jit(solution)/shard_map/psum | solution.py:176
  166.3 65.4 %collective-permute-start.17 = (bf16[3,4,3072]{2,1,0:T(4,128)(2,1)S(1)}, bf16[3,4,3072]{2,1,0:T(4,128)(2,1)S(1)}, u32[]{:S(2)}, u32[]{:S(2)}) collective-permute-start(bf16[3,4,3072]{2,1,0:T(4,128)(2,1)S(1)} %get-tuple-element.118), channel_id=1, source_target_pairs={{0,1},{1,2},{2,3},{3,4},{4,5},{5,6},{6,7},{7,8},{8,9},{9,10},{10,1... | collective-permute-start | bytes 221192 | tf_op jit(solution)/shard_map/ppermute | solution.py:16
  166.3 65.3 %collective-permute-start.18 = (bf16[3,4,3072]{2,1,0:T(4,128)(2,1)S(1)}, bf16[3,4,3072]{2,1,0:T(4,128)(2,1)S(1)}, u32[]{:S(2)}, u32[]{:S(2)}) collective-permute-start(bf16[3,4,3072]{2,1,0:T(4,128)(2,1)S(1)} %get-tuple-element.119), channel_id=1, source_target_pairs={{1,0},{2,1},{3,2},{4,3},{5,4},{6,5},{7,6},{8,7},{9,8},{10,9},{11,1... | collective-permute-start | bytes 221192 | tf_op jit(solution)/shard_map/ppermute | solution.py:18
  171.2 61.2 %copy-start.3 = (bf16[4,4,3072]{2,1,0:T(4,128)(2,1)S(1)}, bf16[4,4,3072]{2,1,0:T(4,128)(2,1)}, u32[]{:S(2)}) copy-start(bf16[4,4,3072]{2,1,0:T(4,128)(2,1)} %param.11) | copy-start | bytes 294916
  171.2 61.2 %copy-start.6 = (f32[1,1,3072]{2,1,0:T(1,128)S(1)}, f32[1,1,3072]{2,1,0:T(1,128)}, u32[]{:S(2)}) copy-start(f32[1,1,3072]{2,1,0:T(1,128)} %copy-done.5) | copy-start | bytes 36868
  (88 other events, 2708.1 us)
Sparse Core Ops, SparseCore 0:
  30.7 41.1 all-gather.1
  95.6 64.2 reduce-scatter.1
  173.3 89.2 all-reduce.4
